TPU v7x, 512 devices: a whole 4x8x8 slice. The times are simulated.
512 devices in a mesh: fsdp: 128 (over z, y, core), rep: 4 (over x).
Axes of the slice: x: 4, y: 8, z: 8, core: 2. Of those that a mesh axis runs over, the one named last changes fastest.
Arguments:
- gradients: float32 [192, 512, 512], P(None, 'fsdp', 'rep'), may hold values from -6 to 6
- moments: float32 [192, 512, 512], P(None, 'fsdp', 'rep')
- second_moments: float32 [192, 512, 512], P(None, 'fsdp', 'rep'), may hold values from 0.05 to 2
- factors: float32 [128, 4, 512, 512], P('fsdp', 'rep')
- owner_of: int32 [192], replicated, may hold values from 0 to 127, as said below
- slot_order: int32 [128, 2], replicated, may hold values from -1 to 191, as said below
Outputs:
- direction: float32 [192, 512, 512], P(None, 'fsdp', 'rep')
- new_moments: float32 [192, 512, 512], P(None, 'fsdp', 'rep')
- new_second_moments: float32 [192, 512, 512], P(None, 'fsdp', 'rep')
- new_factors: float32 [128, 4, 512, 512], P('fsdp', 'rep')
Inputs may be any that keep to these rules, and one draw needn't show every extreme that they name: slot_order[o, k] is the block in slot k of owner o, or -1 if that slot is empty; every block stands in exactly one slot and every owner holds at least one block. owner_of[b] is the owner whose row of slot_order holds b.
All inputs are finite; a program needn't handle non-finite values.
Results may differ from a plain program's by a relative error of at most 0.0003.
Values sent between devices are 32-bit elements; how exact they have to be, the bound alone decides.
A program may use at most 64 MiB of HBM per device.

v0:
```python
import jax
import jax.numpy as jnp
from jax import lax
from jax.sharding import PartitionSpec as P

NS_STEPS = 3


MOMENT_DECAY = 0.9
SECOND_DECAY = 0.95
FACTOR_DECAY = 0.95
DAMPING = 0.1
ADAM_EPSILON = 1e-08
NORM_EPSILON = 1e-06


def inverse_root(factor):
    highest = lax.Precision.HIGHEST
    identity = jnp.eye(factor.shape[0], dtype=jnp.float32)
    damped = factor + DAMPING * identity
    frobenius = jnp.sqrt(jnp.sum(damped * damped) + NORM_EPSILON)
    scaled = damped / frobenius
    root_est = identity
    for sweep in range(NS_STEPS):
        poly_term = (5.0 * identity - scaled) * 0.25
        if sweep == 0:
            root_est = poly_term * frobenius ** (-0.25)
        else:
            root_est = jnp.dot(
                root_est, poly_term, precision=highest, preferred_element_type=jnp.float32
            )
        if sweep + 1 < NS_STEPS:
            poly_square = jnp.dot(
                poly_term, poly_term, precision=highest, preferred_element_type=jnp.float32
            )
            poly_fourth = jnp.dot(
                poly_square, poly_square, precision=highest, preferred_element_type=jnp.float32
            )
            scaled = jnp.dot(
                poly_fourth, scaled, precision=highest, preferred_element_type=jnp.float32
            )
    return root_est


def shards(gradients, moments, second_moments, factors, owner_of, slot_order):
    highest = lax.Precision.HIGHEST
    owners = lax.axis_size("fsdp")
    replica = lax.axis_index("rep")
    block_count, row_count, quarter = gradients.shape
    capacity = slot_order.shape[1]
    new_moment = MOMENT_DECAY * moments + (1.0 - MOMENT_DECAY) * gradients
    new_second = SECOND_DECAY * second_moments + (1.0 - SECOND_DECAY) * gradients * gradients
    adam_step = new_moment / (jnp.sqrt(new_second) + ADAM_EPSILON)
    adam_sq = jnp.sum(adam_step * adam_step, axis=(1, 2))
    slot_blocks = slot_order.T
    filled = slot_blocks >= 0
    safe_slots = jnp.maximum(slot_blocks, 0)
    adam_parts = jnp.where(filled, adam_sq[safe_slots], 0.0)
    full_rows = lax.all_gather(gradients, "rep", axis=2, tiled=True)
    picked = jnp.where(filled[:, :, None, None], full_rows[safe_slots], 0.0)
    payload = picked.reshape(capacity, owners * row_count, full_rows.shape[2])
    received, norm_parts = (
        lax.all_to_all(payload, "fsdp", split_axis=1, concat_axis=1, tiled=True),
        lax.all_to_all(adam_parts, "fsdp", split_axis=1, concat_axis=1, tiled=True),
    )
    my_block = lax.dynamic_index_in_dim(received, replica // 2, 0, keepdims=False)
    which_side = replica % 2
    oriented = jnp.where(which_side == 0, my_block, my_block.T)
    gram_matrix = jnp.dot(
        oriented, oriented.T, precision=highest, preferred_element_type=jnp.float32
    )
    old_factor = factors[0, 0]
    updated = FACTOR_DECAY * old_factor + (1.0 - FACTOR_DECAY) * gram_matrix
    my_root = inverse_root(updated)
    column_start = replica * quarter
    all_roots = lax.all_gather(my_root[None], "rep", axis=0, tiled=True)
    left_roots = all_roots[0::2]
    right_cols = lax.dynamic_slice_in_dim(all_roots[1::2], column_start, quarter, 2)
    pieces = []
    for slot_index in range(capacity):
        right_applied = jnp.dot(
            received[slot_index],
            right_cols[slot_index],
            precision=highest,
            preferred_element_type=jnp.float32,
        )
        pieces.append(
            jnp.dot(
                left_roots[slot_index],
                right_applied,
                precision=highest,
                preferred_element_type=jnp.float32,
            )
        )
    shampoo = jnp.stack(pieces)
    shampoo_parts = jnp.sum(shampoo * shampoo, axis=(1, 2))
    adam_total, shampoo_total = lax.psum((jnp.sum(norm_parts, axis=1), shampoo_parts), "rep")
    graft_scale = jnp.sqrt(adam_total) / jnp.sqrt(shampoo_total + NORM_EPSILON)
    grafted = shampoo * graft_scale[:, None, None]
    returned = lax.all_to_all(grafted, "fsdp", split_axis=1, concat_axis=0, tiled=True)
    block_ids = jnp.arange(block_count, dtype=jnp.int32)
    matches = slot_order[owner_of] == block_ids[:, None]
    slot_of = jnp.sum(jnp.where(matches, jnp.arange(capacity, dtype=jnp.int32)[None, :], 0), axis=1)
    direction = returned[owner_of * capacity + slot_of]
    return (direction, new_moment, new_second, updated[None, None])


def solution(mesh):
    return jax.shard_map(
        shards,
        mesh=mesh,
        in_specs=(
            P(None, "fsdp", "rep"),
            P(None, "fsdp", "rep"),
            P(None, "fsdp", "rep"),
            P("fsdp", "rep", None, None),
            P(),
            P(),
        ),
        out_specs=(
            P(None, "fsdp", "rep"),
            P(None, "fsdp", "rep"),
            P(None, "fsdp", "rep"),
            P("fsdp", "rep", None, None),
        ),
        check_vma=False,
    )
```

profile of v0, /device:TPU:1, one launch (start us, length us, event | category | flops | bytes accessed | tf_op | source)
XLA Modules:
  0.0 264.4 jit_solution(956072499629046263)
XLA Ops:
  7.2 0.0 all-gather.4.cloned.1.call-start
  7.2 0.7 all-gather.4.cloned.1.call-update
  7.9 0.7 maximum_bitcast_fusion
  8.6 3.0 %multiply_reduce_fusion.2 = (f32[192]{0:T(256)S(1)}, f32[192,4,128]{2,1,0:T(4,128)}, f32[192,4,128]{2,1,0:T(4,128)}) fusion(f32[192,4,128]{2,1,0:T(4,128)} %param.6, f32[192,4,128]{2,1,0:T(4,128)} %param.8, f32[192,4,128]{2,1,0:T(4,128)} %param.7), kind=kLoop, calls=%fused_computation.49 | loop fusion | flops 1081152 | bytes 1966848 | tf_op jit(solution)/shard_map/reduce_sum | solution.py:54
  11.6 1.9 gather_fusion.1
  13.6 0.1 broadcast_in_dim.52
  13.7 0.1 broadcast_in_dim.53
  13.9 36.4 %all-gather.4.cloned.1.call-done = f32[192,4,512]{2,1,0:T(4,128)} async-done(((f32[192,4,128]{2,1,0:T(4,128)}), f32[192,4,512]{2,1,0:T(4,128)}) %all-gather.4.cloned.1.call-update) | async-done | bytes 1572880 | tf_op jit(solution)/shard_map/all_gather | solution.py:59
  50.3 3.3 %gather_fusion = f32[256,4,512]{2,1,0:T(4,128)S(1)} fusion(f32[192,4,512]{2,1,0:T(4,128)} %all-gather.4.cloned.1.call-done, s32[1024]{0:T(1024)S(1)} %pad_clamp_fusion.2), kind=kCustom, calls=%fused_computation | custom fusion | bytes 4195328 | tf_op jit(solution)/shard_map/gather | solution.py:60
  53.5 1.8 gather.15
  55.3 1.8 broadcast_select_fusion
  57.1 3.0 %copy.27 = f32[2,512,512]{2,0,1:T(2,128)} copy(f32[2,512,512]{2,1,0:T(8,128)S(1)} %broadcast_select_fusion) | data formatting | bytes 4194304 | tf_op jit(solution)/shard_map/jit(_where)/select_n | solution.py:60
  60.1 15.2 %all-to-all-start = ((f32[2,512,512]{2,0,1:T(2,128)}), f32[2,512,512]{2,0,1:T(2,128)S(1)}, u32[]{:S(2)}, u32[]{:S(2)}) async-start(f32[2,512,512]{2,0,1:T(2,128)} %copy.27), calls=%async_computation | async-start | bytes 4194304 | tf_op jit(solution)/shard_map/all_to_all | solution.py:63
  75.3 0.0 all-gather.6.cloned.1.call-start
  75.3 51.2 %all-to-all-done = f32[2,512,512]{2,0,1:T(2,128)S(1)} async-done(((f32[2,512,512]{2,0,1:T(2,128)}), f32[2,512,512]{2,0,1:T(2,128)S(1)}, u32[]{:S(2)}, u32[]{:S(2)}) %all-to-all-start) | async-done | bytes 2097184 | tf_op jit(solution)/shard_map/all_to_all | solution.py:63
  126.5 3.4 %fusion.48 = (f32[1,512,512]{2,0,1:T(1,128)}, f32[1,512,512]{2,0,1:T(1,128)}, f32[1,512,512]{2,0,1:T(1,128)S(1)}) fusion(f32[2,512,512]{2,0,1:T(2,128)S(1)} %all-to-all-done, s32[]{:T(128)S(6)} %select_n.51), kind=kLoop, calls=%fused_computation.79 | loop fusion | bytes 6291460 | tf_op jit(solution)/shard_map/slice | solution.py:82
  129.9 1.5 copy.38
  131.4 3.5 %multiply_reduce_fusion = (f32[]{:T(128)}, f32[512,512]{1,0:T(8,128)}) fusion(f32[1,512,512]{1,2,0:T(8,128)S(1)} %copy.38, f32[1,512,512]{2,0,1:T(1,128)S(1)} %get-tuple-element.15, pred[]{:T(512)S(6)} %eq.23, f32[1,1,512,512]{3,2,1,0:T(8,128)S(1)} %copy-done.2), kind=kOutput, calls=%fused_computation.27 | convolution fusion | flops 1612972032 | bytes 4194309 | tf_op jit(solution)/shard_map/dot_general | solution.py:69
  135.7 3.8 %fusion.9 = f32[512,512]{1,0:T(8,128)S(1)} fusion(f32[512,512]{1,0:T(8,128)} %get-tuple-element.17, f32[]{:T(128)S(6)} %sqrt.12), kind=kOutput, calls=%fused_computation.23 | convolution fusion | flops 1612447744 | bytes 2097156 | tf_op jit(solution)/shard_map/dot_general | solution.py:33
  139.5 1.8 fusion.49
  141.3 1.9 fusion.43
  143.2 1.9 fusion.14
  145.2 1.8 fusion.50
  147.0 1.8 fusion.1
  148.9 2.3 fusion.11
  151.2 2.8 %fusion.51 = f32[512,512]{1,0:T(8,128)} fusion(f32[512,512]{1,0:T(8,128)S(1)} %fusion.11, f32[512,512]{1,0:T(8,128)S(1)} %fusion.1), kind=kOutput, calls=%fused_computation.82 | convolution fusion | flops 1610612736 | bytes 3145728 | tf_op jit(solution)/shard_map/dot_general | solution.py:29
  154.0 0.7 copy.30
  154.8 8.8 %all-to-all-start.1 = ((f32[2,128,1]{0,2,1:T(1,128)}), f32[2,128,1]{0,2,1:T(1,128)S(1)}, u32[]{:S(2)}, u32[]{:S(2)}) async-start(f32[2,128,1]{0,2,1:T(1,128)} %copy.30), calls=%async_computation.1 | async-start | bytes 131072 | tf_op jit(solution)/shard_map/all_to_all | solution.py:64
  163.6 11.4 %all-to-all-done.1 = f32[2,128,1]{0,2,1:T(1,128)S(1)} async-done(((f32[2,128,1]{0,2,1:T(1,128)}), f32[2,128,1]{0,2,1:T(1,128)S(1)}, u32[]{:S(2)}, u32[]{:S(2)}) %all-to-all-start.1) | async-done | bytes 1056 | tf_op jit(solution)/shard_map/all_to_all | solution.py:64
  175.0 0.2 reduce_sum.47
  175.2 28.2 %all-gather.6.cloned.1.call-done = f32[2048,512]{1,0:T(8,128)} async-done(((f32[512,512]{1,0:T(8,128)}), f32[2048,512]{1,0:T(8,128)}) %all-gather.6.cloned.1.call-update) | async-done | bytes 4194320 | tf_op jit(solution)/shard_map/all_gather | solution.py:76
  203.4 2.8 %fusion.47 = (f32[2,512,512]{2,1,0:T(8,128)S(1)}, f32[2,512,512]{2,1,0:T(8,128)S(1)}) fusion(f32[4,512,512]{2,1,0:T(8,128)} %bitcast.68), kind=kLoop, calls=%fused_computation.78 | loop fusion | bytes 8388608 | tf_op jit(solution)/shard_map/slice | solution.py:77
  206.2 1.0 fusion.6
  207.2 1.0 convolution_bitcast_fusion.1
  208.2 1.0 fusion.3
  209.2 1.0 convolution_bitcast_fusion
  210.2 0.2 multiply_reduce_fusion.1
  210.3 6.5 %all-reduce = (f32[2]{0:T(128)S(1)}, f32[2]{0:T(128)S(1)}) all-reduce(f32[2]{0:T(128)S(1)} %multiply_reduce_fusion.1, f32[2]{0:T(128)S(1)} %reduce_sum.47), channel_id=1, replica_groups=mesh['fsdp'=128,'rep'=4] {'rep'}, use_global_device_ids=true, to_apply=%region_5.6 | all-reduce | flops 4 | bytes 32 | tf_op jit(solution)/shard_map/psum | solution.py:97
  216.9 0.1 fusion.28
  217.0 1.2 copy.31
  218.2 16.6 %all-to-all-start.2 = ((f32[2,512,128]{2,0,1:T(2,128)}), f32[2,512,128]{2,0,1:T(2,128)S(1)}, u32[]{:S(2)}, u32[]{:S(2)}) async-start(f32[2,512,128]{2,0,1:T(2,128)} %copy.31), calls=%async_computation.2 | async-start | bytes 1048576 | tf_op jit(solution)/shard_map/all_to_all | solution.py:100
  234.8 0.1 copy.33
  235.0 0.7 gather_fusion.2
  235.7 0.1 select_reduce_fusion
  235.8 19.6 %all-to-all-done.2 = f32[2,512,128]{2,0,1:T(2,128)S(1)} async-done(((f32[2,512,128]{2,0,1:T(2,128)}), f32[2,512,128]{2,0,1:T(2,128)S(1)}, u32[]{:S(2)}, u32[]{:S(2)}) %all-to-all-start.2) | async-done | bytes 524320 | tf_op jit(solution)/shard_map/all_to_all | solution.py:100
  255.4 0.2 copy.32
  255.6 0.3 copy.34
  255.9 1.6 gather_fusion.3
  (20 shorter events, 0.1 us)
Async XLA Ops:
  7.2 6.4 %copy-start.4 = (s32[128,2]{0,1:T(2,128)S(1)}, s32[128,2]{0,1:T(2,128)}, u32[]{:S(2)}) copy-start(s32[128,2]{0,1:T(2,128)} %param.11) | copy-start | bytes 3076
  7.2 43.1 %all-gather.4.cloned.1.call-start = ((), (), s32[]{:S(2)}) async-start(), calls=%async_computation.3 | async-start | bytes 1966080 | tf_op jit(solution)/shard_map/all_gather | solution.py:59
  60.1 66.4 %all-to-all-start = ((f32[2,512,512]{2,0,1:T(2,128)}), f32[2,512,512]{2,0,1:T(2,128)S(1)}, u32[]{:S(2)}, u32[]{:S(2)}) async-start(f32[2,512,512]{2,0,1:T(2,128)} %copy.27), calls=%async_computation | async-start | bytes 4194304 | tf_op jit(solution)/shard_map/all_to_all | solution.py:63
  75.3 128.1 %all-gather.6.cloned.1.call-start = ((), (), s32[]{:S(2)}) async-start(), calls=%async_computation.4 | async-start | bytes 5242880 | tf_op jit(solution)/shard_map/all_gather | solution.py:76
  129.9 1.5 copy-start.2
  139.5 1.9 copy-start.3
  154.8 20.2 %all-to-all-start.1 = ((f32[2,128,1]{0,2,1:T(1,128)}), f32[2,128,1]{0,2,1:T(1,128)S(1)}, u32[]{:S(2)}, u32[]{:S(2)}) async-start(f32[2,128,1]{0,2,1:T(1,128)} %copy.30), calls=%async_computation.1 | async-start | bytes 131072 | tf_op jit(solution)/shard_map/all_to_all | solution.py:64
  203.4 2.8 %copy-start.1 = (f32[1,512,512]{2,0,1:T(1,128)S(1)}, f32[1,512,512]{2,0,1:T(1,128)}, u32[]{:S(2)}) copy-start(f32[1,512,512]{2,0,1:T(1,128)} %get-tuple-element.13) | copy-start | bytes 3145732
  206.1 2.0 copy-start
  210.2 24.8 %copy-start.5 = (s32[192]{0:T(256)S(1)}, s32[192]{0:T(256)}, u32[]{:S(2)}) copy-start(s32[192]{0:T(256)} %param.10) | copy-start | bytes 2308
  218.2 37.2 %all-to-all-start.2 = ((f32[2,512,128]{2,0,1:T(2,128)}), f32[2,512,128]{2,0,1:T(2,128)S(1)}, u32[]{:S(2)}, u32[]{:S(2)}) async-start(f32[2,512,128]{2,0,1:T(2,128)} %copy.31), calls=%async_computation.2 | async-start | bytes 1048576 | tf_op jit(solution)/shard_map/all_to_all | solution.py:100
Sparse Core Ops, SparseCore 0:
  10.1 40.1 all-gather.3
  154.2 49.1 all-gather.5
where the time goes:
time: 265 us; the launch traced here: 264 us
  waiting for transfers between devices  147 us (55%)
  starting transfers between devices  40.7 us (15%)
  matrix products  25.7 us (10%)
  local copies, waits for them, and re-layouts  22.8 us (9%)
  between operations  15.1 us (6%)
  blocking collectives  6.54 us (2%)
  other arithmetic  6.13 us (2%)
    all_to_all x1, waiting for transfers between devices, shards(): lax.all_to_all(payload, 'fsdp', split_axis=1, concat_axis=1, tiled=True)  51.2 us
    all_gather x1, waiting for transfers between devices, shards(): full_rows = lax.all_gather(gradients, 'rep', axis=2, tiled=True)  36.4 us
    all_gather x1, waiting for transfers between devices, shards(): all_roots = lax.all_gather(my_root[None], 'rep', axis=0, tiled=True)  28.2 us
    all_to_all x1, waiting for transfers between devices, shards(): lax.all_to_all(grafted, 'fsdp', split_axis=1, concat_axis=0, tiled=True)  19.6 us
    all_to_all x1, starting transfers between devices, shards(): lax.all_to_all(grafted, 'fsdp', split_axis=1, concat_axis=0, tiled=True)  16.6 us
    all_to_all x1, starting transfers between devices, shards(): lax.all_to_all(payload, 'fsdp', split_axis=1, concat_axis=1, tiled=True)  15.2 us
    all_to_all x1, waiting for transfers between devices, shards(): lax.all_to_all(adam_parts, 'fsdp', split_axis=1, concat_axis=1, tiled=True)  11.4 us
    all_to_all x1, starting transfers between devices, shards(): lax.all_to_all(adam_parts, 'fsdp', split_axis=1, concat_axis=1, tiled=True)  8.85 us
  transfers between devices with their start and end apart: 5, of which 5 were waited for; matrix products, arithmetic and copies ran while one was open for 3% of the time, Pallas kernels for 0%

commit v1 on v0

v1 whole, which is shorter than its diff:
```python
import jax
import jax.numpy as jnp
from jax import lax
from jax.experimental import pallas as pl
from jax.experimental.pallas import tpu as pltpu
from jax.sharding import PartitionSpec as P

MOMENT_DECAY = 0.9
SECOND_DECAY = 0.95
FACTOR_DECAY = 0.95
DAMPING = 0.1
ADAM_EPSILON = 1e-08
NORM_EPSILON = 1e-06

BLOCK = 512
OWNERS = 128
BLOCKS = 192
MESH = pl.DeviceIdType.MESH
f32 = jnp.float32
bf16 = jnp.bfloat16


def split(x):
    hi = x.astype(bf16)
    return hi, (x - hi.astype(f32)).astype(bf16)


def mm(a, b, dims=((1,), (0,))):
    (ah, al), (bh, bl) = a, b

    def dot(x, y):
        return lax.dot_general(x, y, (dims, ((), ())), preferred_element_type=f32)

    return dot(ah, bh) + (dot(ah, bl) + dot(al, bh))


def damp(factor, eye):
    damped = factor + DAMPING * eye
    frobenius = jnp.sqrt(jnp.sum(damped * damped, keepdims=True) + NORM_EPSILON)
    return damped * (1.0 / frobenius), frobenius


def root_steps(factor, eye):
    m, c = damp(factor, eye)
    ms = split(m)
    n = mm(ms, ms)
    q = split(1.5625 * eye - 0.625 * m + 0.0625 * n)
    yield
    q = split(mm(q, q))
    yield
    m1 = mm(q, ms)
    m1s = split(m1)
    yield
    n1 = mm(m1s, m1s)
    p = split(1.5625 * eye - 0.625 * m1 + 0.0625 * n1)
    w = split(1.25 * m1 - 0.25 * n1)
    yield
    p = split(mm(p, p))
    yield
    y = mm(p, w)
    u = split(1.5625 * eye - 0.3125 * m1 - 0.25 * y)
    t0 = split((1.25 * eye - 0.25 * m) * lax.rsqrt(jnp.sqrt(c)))
    yield
    yield split(mm(t0, u))


def run(gen):
    last = None
    for last in gen:
        pass
    return last


def remote(src, dst, send, recv, device):
    return pltpu.make_async_remote_copy(
        src_ref=src, dst_ref=dst, send_sem=send, recv_sem=recv, device_id=device, device_id_type=MESH
    )


def wrap(v, n):
    return jnp.where(v >= n, v - n, v)


def kernel(
    slot_ref, owner_ref, g_ref, m_ref, v_ref, f_ref,
    dir_ref, nm_ref, nv_ref, nf_ref,
    pay, gq, other, fresh, xq, xs, ret, eye_ref, g_full, sums, part, ga, gz, gx,
    stage, send1, recv1, fsend, frecv, usend, urecv, spsend, sprecv, send2, recv2,
    asend, arecv,
):
    me = lax.axis_index("fsdp")
    rep = lax.axis_index("rep")
    z = me // 16
    yc = me - z * 16
    site = lax.rem(rep, 2) == 0
    slot = rep // 2

    barrier = pltpu.get_barrier_semaphore()

    def signal(sem, d, r):
        pl.semaphore_signal(sem, inc=1, device_id=(d, r), device_id_type=MESH)

    for t in range(4):
        for s in range(0 if t else 1, 16):
            signal(barrier, z * 16 + wrap(yc + s, 16), wrap(rep + t, 4))
    for s in range(1, 8):
        signal(barrier, wrap(z + s, 8) * 16 + yc, rep)

    def pick(o, carry):
        for k in range(2):
            b = slot_ref[2 * o + k]
            chunk = g_ref[jnp.maximum(b, 0)]
            pay[k, o] = jnp.where(b >= 0, chunk, 0.0)
        return carry

    lax.fori_loop(0, OWNERS, pick, 0, unroll=8)

    pl.semaphore_wait(barrier, 70)
    for s in range(1, 8):
        signal(stage, wrap(z + s, 8) * 16 + yc, rep)
    pl.semaphore_wait(stage, 7)

    def send(s, carry):
        d = lax.rem(me + s * 37, OWNERS)
        for k in range(2):
            remote(pay.at[k, d], gq.at[rep, me // 2, lax.rem(me, 2)], send1, recv1.at[rep], (d, 2 * k)).start()
        return carry

    lax.fori_loop(1, OWNERS, send, 0, unroll=4)
    for k in range(2):
        own_chunk = gq.at[rep, me // 2, lax.rem(me, 2)]

        @pl.when(rep != 2 * k)
        def _():
            remote(pay.at[k, me], own_chunk, send1, recv1.at[rep], (me, 2 * k)).start()

        @pl.when(rep == 2 * k)
        def _():
            pltpu.make_async_copy(pay.at[k, me], own_chunk, recv1.at[rep]).start()

    @pl.when(jnp.logical_not(site))
    def _():
        remote(f_ref, other, fsend, frecv, (me, rep - 1)).start()

    grad = g_ref[...]
    new_m = MOMENT_DECAY * m_ref[...] + (1.0 - MOMENT_DECAY) * grad
    new_v = SECOND_DECAY * v_ref[...] + (1.0 - SECOND_DECAY) * grad * grad
    nm_ref[...] = new_m
    nv_ref[...] = new_v
    adam = new_m / (jnp.sqrt(new_v) + ADAM_EPSILON)
    rows = jnp.sum(adam * adam, axis=1)
    part[...] = jnp.zeros_like(part)
    part[0:BLOCKS, :] = rows
    total = lax.dot_general(
        jnp.ones((8, 128), f32), part[...], (((1,), (1,)), ((), ())),
        precision=lax.Precision.HIGHEST, preferred_element_type=f32,
    )[0:1]

    def share(buf, step, here, n, device):
        buf[here] = sums_of[0]
        for s in range(1, n):
            remote(buf.at[here], buf.at[here], asend.at[step], arecv.at[step], device(s)).start()
        some = buf.at[pl.ds(0, n - 1)]
        pltpu.make_async_copy(some, some, asend.at[step]).wait()
        pltpu.make_async_copy(some, some, arecv.at[step]).wait()
        out = buf[0]
        for s in range(1, n):
            out = out + buf[s]
        sums_of[0] = out

    sums_of = [total]
    share(ga, 0, yc, 16, lambda s: (z * 16 + wrap(yc + s, 16), rep))
    share(gz, 1, z, 8, lambda s: (wrap(z + s, 8) * 16 + yc, rep))
    share(gx, 2, rep, 4, lambda s: (me, wrap(rep + s, 4)))
    sums[...] = sums_of[0]

    pltpu.make_async_copy(pay.at[:, pl.ds(0, 127)], pay.at[:, pl.ds(0, 127)], send1).wait()
    for k in range(2):
        @pl.when(rep != 2 * k)
        def _():
            pltpu.make_async_copy(pay.at[k, 0], pay.at[k, 0], send1).wait()

    @pl.when(site)
    def _():
        row = lax.broadcasted_iota(jnp.int32, (BLOCK, BLOCK), 0)
        col = lax.broadcasted_iota(jnp.int32, (BLOCK, BLOCK), 1)
        eye_ref[...] = jnp.where(row == col, 1.0, 0.0)
        for q in range(4):
            pltpu.make_async_copy(gq.at[q], gq.at[q], recv1.at[q]).wait()
        for q in range(4):
            both = jnp.concatenate([gq[q, :, 0], gq[q, :, 1]], axis=1)
            g_full[:, q * 128 : (q + 1) * 128] = both.reshape(BLOCK, 128)
        gs = split(g_full[...])
        left_gram = mm(gs, gs, ((1,), (1,)))
        left = FACTOR_DECAY * f_ref[...] + (1.0 - FACTOR_DECAY) * left_gram
        nf_ref[...] = left
        left_root = run(root_steps(left, eye_ref[...]))
        applied = split(mm(left_root, gs))
        right_gram = mm(gs, gs, ((0,), (0,)))
        remote(f_ref, other, fsend, frecv, (me, rep + 1)).wait_recv()
        right = FACTOR_DECAY * other[...] + (1.0 - FACTOR_DECAY) * right_gram
        fresh[...] = right
        remote(fresh, nf_ref, usend, urecv, (me, rep + 1)).start()
        right_root = run(root_steps(right, eye_ref[...]))
        shampoo = mm(applied, right_root)
        b = slot_ref[2 * me + slot]
        lane = lax.broadcasted_iota(jnp.int32, sums.shape, 1)
        adam_total = jnp.sum(jnp.where(lane == b, sums[...], 0.0), keepdims=True)
        shampoo_total = jnp.sum(shampoo * shampoo, keepdims=True)
        scale = jnp.sqrt(adam_total) / jnp.sqrt(shampoo_total + NORM_EPSILON)
        for q in range(4):
            part_q = (shampoo[:, q * 128 : (q + 1) * 128] * scale).reshape(64, 8, 128)
            xq[q, :, 0] = part_q[:, 0:4]
            xq[q, :, 1] = part_q[:, 4:8]
        for c in range(4):
            @pl.when(rep != c)
            def _():
                remote(xq.at[c], xs.at[slot], spsend, sprecv.at[slot], (me, c)).start()

            @pl.when(rep == c)
            def _():
                pltpu.make_async_copy(xq.at[c], xs.at[slot], sprecv.at[slot]).start()

    for k in range(2):
        pltpu.make_async_copy(xs.at[k], xs.at[k], sprecv.at[k]).wait()

    def give(s, carry):
        d = lax.rem(me + s * 37, OWNERS)
        remote(xs.at[:, d // 2, lax.rem(d, 2)], ret.at[:, me], send2, recv2, (d, rep)).start()
        return carry

    lax.fori_loop(1, OWNERS, give, 0, unroll=4)
    pltpu.make_async_copy(xs.at[:, me // 2, lax.rem(me, 2)], ret.at[:, me], recv2).start()
    pltpu.make_async_copy(pay.at[:, pl.ds(0, 127)], pay.at[:, pl.ds(0, 127)], send2).wait()
    pltpu.make_async_copy(ret, ret, recv2).wait()

    def place(b, carry):
        o = owner_ref[b]
        k = jnp.where(slot_ref[2 * o] == b, 0, 1)
        dir_ref[b] = ret[k, o]
        return carry

    lax.fori_loop(0, BLOCKS, place, 0, unroll=8)

    @pl.when(site)
    def _():
        remote(fresh, nf_ref, usend, urecv, (me, rep + 1)).wait_send()
        pltpu.make_async_copy(xq.at[pl.ds(0, 3)], xq.at[pl.ds(0, 3)], spsend).wait()

    @pl.when(jnp.logical_not(site))
    def _():
        remote(f_ref, other, fsend, frecv, (me, rep - 1)).wait_send()
        remote(fresh, nf_ref, usend, urecv, (me, rep - 1)).wait_recv()


def shards(gradients, moments, second_moments, factors, owner_of, slot_order):
    vmem = pl.BlockSpec(memory_space=pltpu.VMEM)
    smem = pl.BlockSpec(memory_space=pltpu.SMEM)
    part = jax.ShapeDtypeStruct(gradients.shape, f32)
    chunks = lambda n: pltpu.VMEM((n, OWNERS, 4, 128), f32)
    halves = lambda n: pltpu.VMEM((n, 64, 2, 4, 128), f32)
    square = pltpu.VMEM((BLOCK, BLOCK), f32)
    dma = pltpu.SemaphoreType.DMA
    direction, new_m, new_v, new_f = pl.pallas_call(
        kernel,
        out_shape=(part, part, part, jax.ShapeDtypeStruct((BLOCK, BLOCK), f32)),
        in_specs=[smem, smem, vmem, vmem, vmem, vmem],
        out_specs=(vmem, vmem, vmem, vmem),
        scratch_shapes=[
            chunks(2), halves(4), square, square, halves(4), halves(2), chunks(2), square, square,
            pltpu.VMEM((1, 256), f32), pltpu.VMEM((256, 128), f32),
            pltpu.VMEM((16, 1, 256), f32), pltpu.VMEM((8, 1, 256), f32), pltpu.VMEM((4, 1, 256), f32),
            pltpu.SemaphoreType.REGULAR, dma, dma((4,)), dma, dma, dma, dma, dma, dma((2,)), dma, dma,
            dma((3,)), dma((3,)),
        ],
        compiler_params=pltpu.CompilerParams(
            collective_id=0, has_side_effects=True, vmem_limit_bytes=56 << 20
        ),
    )(slot_order.reshape(-1), owner_of, gradients, moments, second_moments, factors.reshape(BLOCK, BLOCK))
    return direction, new_m, new_v, new_f[None, None]


def solution(mesh):
    split_blocks = P(None, "fsdp", "rep")
    return jax.shard_map(
        shards,
        mesh=mesh,
        in_specs=(split_blocks, split_blocks, split_blocks, P("fsdp", "rep", None, None), P(), P()),
        out_specs=(split_blocks, split_blocks, split_blocks, P("fsdp", "rep", None, None)),
        check_vma=False,
    )
```

time: 265 us -> 127 us (0.48)
  the two profiles are of different devices: /device:TPU:1 before, /device:TPU:13 now
where the time goes in v1:
time: 127 us
  Pallas kernels  119 us (94%)
  local copies, waits for them, and re-layouts  6.88 us (5%)
    pallas_call x1, Pallas kernels, shards(): pl.pallas_call(kernel, out_shape=(part, part, part, jax.ShapeDtypeStruct(...  119 us
    unnamed x11, local copies, waits for them, and re-layouts  6.18 us

profile of v1, /device:TPU:13, one launch (start us, length us, event | category | flops | bytes accessed | tf_op | source)
XLA Modules:
  0.0 126.8 jit_solution(6029483408900621526)
XLA Ops:
  0.6 0.0 copy-start.2
  0.6 0.7 copy-done.2
  1.3 0.1 copy.10
  1.4 0.7 reshape.14.slot_ref
  2.1 119.3 %shard_map.93 = (f32[192,4,128]{2,1,0:T(4,128)}, f32[192,4,128]{2,1,0:T(4,128)}, f32[192,4,128]{2,1,0:T(4,128)}, f32[512,512]{1,0:T(8,128)}) custom-call(s32[256]{0:T(256)} %reshape.14.slot_ref, s32[192]{0:T(256)} %owner_ref.1, f32[192,4,128]{2,1,0:T(4,128)} %g_ref.1, f32[192,4,128]{2,1,0:T(4,128)} %m_ref.1, f32[192,4,128]{2,1,0:T(4,128)} %v_ref.1, ...), custom_call_target="tpu_custom_call" | custom-call | tf_op jit(solution)/shard_map/pallas_call | solution.py:264
  121.4 0.0 copy-start
  121.4 1.9 %copy.15 = f32[192,4,128]{2,1,0:T(4,128)} copy(f32[192,4,128]{2,1,0:T(4,128)} %get-tuple-element.16) | data formatting | bytes 786432
  123.3 0.0 copy-start.1
  123.3 1.8 %copy.16 = f32[192,4,128]{2,1,0:T(4,128)} copy(f32[192,4,128]{2,1,0:T(4,128)} %get-tuple-element.17) | data formatting | bytes 786432
  125.1 0.0 copy-done.1
  125.1 0.7 copy.17
  125.8 0.0 copy-done
  125.8 1.0 copy.18
Async XLA Ops:
  0.6 0.7 copy-start.2
  121.4 4.4 %copy-start = (f32[512,512]{1,0:T(8,128)S(1)}, f32[512,512]{1,0:T(8,128)}, u32[]{:S(2)}) copy-start(f32[512,512]{1,0:T(8,128)} %get-tuple-element.11) | copy-start | bytes 3145732
  123.3 1.8 %copy-start.1 = (f32[192,4,128]{2,1,0:T(4,128)S(1)}, f32[192,4,128]{2,1,0:T(4,128)}, u32[]{:S(2)}) copy-start(f32[192,4,128]{2,1,0:T(4,128)} %get-tuple-element.18) | copy-start | bytes 1179652

commit v2 on v1

v2 whole, which is shorter than its diff:
```python
import functools

import jax
import jax.numpy as jnp
from jax import lax
from jax.experimental import pallas as pl
from jax.experimental.pallas import tpu as pltpu
from jax.sharding import PartitionSpec as P

MOMENT_DECAY = 0.9
SECOND_DECAY = 0.95
FACTOR_DECAY = 0.95
DAMPING = 0.1
ADAM_EPSILON = 1e-08
NORM_EPSILON = 1e-06

BLOCK = 512
OWNERS = 128
BLOCKS = 192
MESH = pl.DeviceIdType.MESH
DIRECT = (0, 4)
PHASES = ((1, 2, 3), (5, 6, 7))
RELAYED = 16 * sum(len(p) for p in PHASES)
f32 = jnp.float32
bf16 = jnp.bfloat16


def split(x):
    hi = x.astype(bf16)
    return hi, (x - hi.astype(f32)).astype(bf16)


def mm(a, b, dims=((1,), (0,))):
    (ah, al), (bh, bl) = a, b

    def dot(x, y):
        return lax.dot_general(x, y, (dims, ((), ())), preferred_element_type=f32)

    return dot(ah, bh) + (dot(ah, bl) + dot(al, bh))


def damp(factor, eye):
    damped = factor + DAMPING * eye
    frobenius = jnp.sqrt(jnp.sum(damped * damped, keepdims=True) + NORM_EPSILON)
    return damped * (1.0 / frobenius), frobenius


def root_steps(factor, eye):
    m, c = damp(factor, eye)
    ms = split(m)
    n = mm(ms, ms)
    q = split(1.5625 * eye - 0.625 * m + 0.0625 * n)
    yield
    q = split(mm(q, q))
    yield
    m1 = mm(q, ms)
    m1s = split(m1)
    yield
    n1 = mm(m1s, m1s)
    p = split(1.5625 * eye - 0.625 * m1 + 0.0625 * n1)
    w = split(1.25 * m1 - 0.25 * n1)
    yield
    p = split(mm(p, p))
    yield
    y = mm(p, w)
    u = split(1.5625 * eye - 0.3125 * m1 - 0.25 * y)
    t0 = split((1.25 * eye - 0.25 * m) * lax.rsqrt(jnp.sqrt(c)))
    yield
    yield split(mm(t0, u))


def run(gen):
    last = None
    for last in gen:
        pass
    return last


def remote(src, dst, send, recv, device):
    return pltpu.make_async_remote_copy(
        src_ref=src, dst_ref=dst, send_sem=send, recv_sem=recv, device_id=device, device_id_type=MESH
    )


def wrap(v, n):
    return jnp.where(v >= n, v - n, v)


def kernel(
    slot_ref, owner_ref, g_ref, m_ref, v_ref, f_ref,
    dir_ref, nm_ref, nv_ref, nf_ref,
    pay, gq, other, gram, xq, xs, ret, eye_ref, g_full, sums, part, ga, gz, gx,
    inside, stage2, stage3, stage4, go2, go3,
    send1, recv1, fsend, frecv, usend, urecv, spsend, sprecv, send2, recv2, asend, arecv,
):
    me = lax.axis_index("fsdp")
    rep = lax.axis_index("rep")
    z = me // 16
    yc = me - z * 16
    site = lax.rem(rep, 2) == 0
    odd = jnp.logical_not(site)
    slot = rep // 2
    twin = wrap(rep + 2, 4)

    barrier = pltpu.get_barrier_semaphore()

    def signal(sem, d, r):
        pl.semaphore_signal(sem, inc=1, device_id=(d, r), device_id_type=MESH)

    @pl.when(site)
    def _():
        signal(barrier, me, rep + 1)
        for t in range(2):
            for s in range(0 if t else 1, 16):
                signal(barrier, z * 16 + wrap(yc + s, 16), wrap(rep + 2 * t, 4))
            for s in range(1, 8):
                signal(barrier, wrap(z + s, 8) * 16 + yc, wrap(rep + 2 * t, 4))

    @pl.when(odd)
    def _():
        pl.semaphore_wait(barrier, 1)
        remote(f_ref, other, fsend, frecv, (me, rep - 1)).start()
        signal(inside, me, rep - 1)

    def pick(o, carry):
        for k in range(2):
            b = slot_ref[k, o]
            chunk = g_ref[jnp.maximum(b, 0)]
            pay[k, o] = jnp.where(b >= 0, chunk, 0.0)
        return carry

    lax.fori_loop(0, OWNERS, pick, 0, unroll=8)

    @pl.when(site)
    def _():
        pl.semaphore_wait(barrier, 45)
        pl.semaphore_wait(inside, 1)
        for s in range(1, 16):
            signal(stage2, z * 16 + wrap(yc + s, 16), rep)
        pl.semaphore_wait(stage2, 15)
        signal(go2, me, rep + 1)

    @pl.when(odd)
    def _():
        pl.semaphore_wait(go2, 1)

    def send(s, carry):
        d = lax.rem(me + s * 37, OWNERS)
        for k in range(2):
            remote(pay.at[k, d], gq.at[rep, me // 2, lax.rem(me, 2)], send1, recv1.at[rep], (d, 2 * k)).start()
        return carry

    lax.fori_loop(1, OWNERS, send, 0, unroll=4)
    for k in range(2):
        own_chunk = gq.at[rep, me // 2, lax.rem(me, 2)]

        @pl.when(rep != 2 * k)
        def _():
            remote(pay.at[k, me], own_chunk, send1, recv1.at[rep], (me, 2 * k)).start()

        @pl.when(rep == 2 * k)
        def _():
            pltpu.make_async_copy(pay.at[k, me], own_chunk, recv1.at[rep]).start()

    @pl.when(site)
    def _():
        for s in range(1, 8):
            signal(stage3, wrap(z + s, 8) * 16 + yc, rep)
        pl.semaphore_wait(stage3, 7)
        signal(stage4, me, twin)
        pl.semaphore_wait(stage4, 1)
        signal(go3, me, rep + 1)

    @pl.when(odd)
    def _():
        pl.semaphore_wait(go3, 1)

    grad = g_ref[...]
    new_m = MOMENT_DECAY * m_ref[...] + (1.0 - MOMENT_DECAY) * grad
    new_v = SECOND_DECAY * v_ref[...] + (1.0 - SECOND_DECAY) * grad * grad
    nm_ref[...] = new_m
    nv_ref[...] = new_v
    adam = new_m / (jnp.sqrt(new_v) + ADAM_EPSILON)
    rows = jnp.sum(adam * adam, axis=1)
    part[...] = jnp.zeros_like(part)
    part[0:BLOCKS, :] = rows
    total = lax.dot_general(
        jnp.ones((8, 128), f32), part[...], (((1,), (1,)), ((), ())),
        precision=lax.Precision.HIGHEST, preferred_element_type=f32,
    )[0:1]

    def z_peer(s):
        return wrap(z + s, 8) * 16 + yc

    def y_peer(s):
        return z * 16 + wrap(yc + s, 16)

    def share(buf, step, here, n, value, peer):
        buf[here] = value
        for s in range(1, n):
            remote(buf.at[here], buf.at[here], asend.at[step], arecv.at[step], (peer(s), rep)).start()

    def shared(buf, step, n):
        some = buf.at[pl.ds(0, n - 1)]
        pltpu.make_async_copy(some, some, asend.at[step]).wait()
        pltpu.make_async_copy(some, some, arecv.at[step]).wait()
        return functools.reduce(lambda x, y: x + y, [buf[s] for s in range(n)])

    share(ga, 0, yc, 16, total, y_peer)

    def share_z():
        share(gz, 1, z, 8, shared(ga, 0, 16), z_peer)

    def share_x():
        gx[rep] = shared(gz, 1, 8)

        @pl.when(odd)
        def _():
            for k in range(2):
                remote(gx.at[rep], gx.at[rep], asend.at[2], arecv.at[2], (me, 2 * k)).start()

        @pl.when(site)
        def _():
            remote(gx.at[rep], gx.at[rep], asend.at[3], arecv.at[2], (me, twin)).start()

    @pl.when(odd)
    def _():
        share_z()
        share_x()

    def units(n, sem):
        while n > 0:
            some = xq.at[0, pl.ds(0, min(n, 64))]
            pltpu.make_async_copy(some, some, sem).wait()
            n -= 64

    def group(dz):
        return pl.ds(wrap(z + dz, 8) * 8, 8)

    def each(dzs, act):
        for dz in dzs:
            base = wrap(z + dz, 8) * 16
            if dz == 0:
                act(me, True)

            def body(j, carry):
                act(base + wrap(yc + j, 16), False)
                return carry

            lax.fori_loop(1 if dz == 0 else 0, 16, body, 0, unroll=4 if dz else 3)

    @pl.when(site)
    def _():
        row = lax.broadcasted_iota(jnp.int32, (BLOCK, BLOCK), 0)
        col = lax.broadcasted_iota(jnp.int32, (BLOCK, BLOCK), 1)
        eye_ref[...] = jnp.where(row == col, 1.0, 0.0)
        for q in range(4):
            pltpu.make_async_copy(gq.at[q], gq.at[q], recv1.at[q]).wait()
        for q in range(4):
            both = jnp.concatenate([gq[q, :, 0], gq[q, :, 1]], axis=1)
            g_full[:, q * 128 : (q + 1) * 128] = both.reshape(BLOCK, 128)
        gs = split(g_full[...])
        gram[...] = mm(gs, gs, ((0,), (0,)))
        for i in range(4):
            panel = gram.at[pl.ds(128 * i, 128), pl.ds(128 * i, BLOCK - 128 * i)]
            there = other.at[pl.ds(128 * i, 128), pl.ds(128 * i, BLOCK - 128 * i)]
            remote(panel, there, usend.at[i], urecv.at[i], (me, rep + 1)).start()
        left_gram = mm(gs, gs, ((1,), (1,)))
        left = FACTOR_DECAY * f_ref[...] + (1.0 - FACTOR_DECAY) * left_gram
        nf_ref[...] = left
        share_z()
        left_root = run(root_steps(left, eye_ref[...]))
        applied = split(mm(left_root, gs))
        share_x()
        remote(f_ref, other, fsend, frecv, (me, rep + 1)).wait_recv()
        right = FACTOR_DECAY * other[...] + (1.0 - FACTOR_DECAY) * gram[...]
        right_root = run(root_steps(right, eye_ref[...]))
        shampoo = mm(applied, right_root)
        remote(gx.at[rep], gx.at[rep], asend.at[3], arecv.at[2], (me, twin)).wait_send()
        pltpu.make_async_copy(gx.at[pl.ds(0, 3)], gx.at[pl.ds(0, 3)], arecv.at[2]).wait()
        sums[...] = gx[0] + gx[1] + gx[2] + gx[3]
        b = slot_ref[slot, me]
        lane = lax.broadcasted_iota(jnp.int32, sums.shape, 1)
        adam_total = jnp.sum(jnp.where(lane == b, sums[...], 0.0), keepdims=True)
        shampoo_total = jnp.sum(shampoo * shampoo, keepdims=True)
        scale = jnp.sqrt(adam_total) / jnp.sqrt(shampoo_total + NORM_EPSILON)
        for q in range(4):
            part_q = (shampoo[:, q * 128 : (q + 1) * 128] * scale).reshape(64, 8, 128)
            xq[q, :, 0] = part_q[:, 0:4]
            xq[q, :, 1] = part_q[:, 4:8]
        for phase, dzs in enumerate(PHASES):
            for dz in dzs:
                for c in (1, 3):
                    remote(xq.at[c, group(dz)], xs.at[slot, group(dz)], spsend, sprecv.at[slot, phase], (me, c)).start()

        def own(d, same):
            chunk = xq.at[rep, d // 2, lax.rem(d, 2)]
            if same:
                pltpu.make_async_copy(chunk, ret.at[slot, me], recv2).start()
            else:
                remote(chunk, ret.at[slot, me], send2, recv2, (d, rep)).start()

        def across(d, same):
            remote(xq.at[twin, d // 2, lax.rem(d, 2)], ret.at[slot, me], send2, recv2, (d, twin)).start()

        def aside(d, same):
            for c in (1, 3):
                remote(xq.at[c, d // 2, lax.rem(d, 2)], ret.at[slot, me], send2, recv2, (d, c)).start()

        each(range(8), own)
        each(range(8), across)
        each(DIRECT, aside)
        units(RELAYED, spsend)
        units(127 + 16 * len(DIRECT), send2)
        one = pay.at[0, 0]
        pltpu.make_async_copy(one, one, send2).wait()

    @pl.when(odd)
    def _():
        for i in range(4):
            there = other.at[pl.ds(128 * i, 128), pl.ds(128 * i, BLOCK - 128 * i)]
            remote(there, there, usend.at[i], urecv.at[i], (me, rep - 1)).wait_recv()
        for i in range(4):
            for j in range(4):
                a, b = slice(128 * i, 128 * i + 128), slice(128 * j, 128 * j + 128)
                square = other[a, b] if i <= j else other[b, a].T
                nf_ref[a, b] = FACTOR_DECAY * f_ref[a, b] + (1.0 - FACTOR_DECAY) * square

        def give(d, same):
            chunk = xs.at[:, d // 2, lax.rem(d, 2)]
            if same:
                pltpu.make_async_copy(chunk, ret.at[:, me], recv2).start()
            else:
                remote(chunk, ret.at[:, me], send2, recv2, (d, rep)).start()

        for phase, dzs in enumerate(PHASES):
            some = xs.at[0, pl.ds(0, 8 * len(dzs))]
            for k in range(2):
                pltpu.make_async_copy(some, some, sprecv.at[k, phase]).wait()
            each(dzs, give)
        units(RELAYED, send2)
        pair = gx.at[pl.ds(0, 2)]
        pltpu.make_async_copy(pair, pair, asend.at[2]).wait()
        remote(f_ref, other, fsend, frecv, (me, rep - 1)).wait_send()

    pltpu.make_async_copy(pay.at[:, pl.ds(0, 127)], pay.at[:, pl.ds(0, 127)], send1).wait()
    for k in range(2):
        @pl.when(rep != 2 * k)
        def _():
            pltpu.make_async_copy(pay.at[k, 0], pay.at[k, 0], send1).wait()

    pltpu.make_async_copy(ret, ret, recv2).wait()

    def place(b, carry):
        o = owner_ref[b]
        k = jnp.where(slot_ref[0, o] == b, 0, 1)
        dir_ref[b] = ret[k, o]
        return carry

    lax.fori_loop(0, BLOCKS, place, 0, unroll=8)

    @pl.when(site)
    def _():
        for i in range(4):
            panel = gram.at[pl.ds(128 * i, 128), pl.ds(128 * i, BLOCK - 128 * i)]
            remote(panel, panel, usend.at[i], urecv.at[i], (me, rep + 1)).wait_send()


def shards(gradients, moments, second_moments, factors, owner_of, slot_order):
    vmem = pl.BlockSpec(memory_space=pltpu.VMEM)
    smem = pl.BlockSpec(memory_space=pltpu.SMEM)
    part = jax.ShapeDtypeStruct(gradients.shape, f32)
    chunks = lambda n: pltpu.VMEM((n, OWNERS, 4, 128), f32)
    halves = lambda n: pltpu.VMEM((n, 64, 2, 4, 128), f32)
    square = pltpu.VMEM((BLOCK, BLOCK), f32)
    dma = pltpu.SemaphoreType.DMA
    regular = pltpu.SemaphoreType.REGULAR
    direction, new_m, new_v, new_f = pl.pallas_call(
        kernel,
        out_shape=(part, part, part, jax.ShapeDtypeStruct((BLOCK, BLOCK), f32)),
        in_specs=[smem, smem, vmem, vmem, vmem, vmem],
        out_specs=(vmem, vmem, vmem, vmem),
        scratch_shapes=[
            chunks(2), halves(4), square, square, halves(4), halves(2), chunks(2), square, square,
            pltpu.VMEM((1, 256), f32), pltpu.VMEM((256, 128), f32),
            pltpu.VMEM((16, 1, 256), f32), pltpu.VMEM((8, 1, 256), f32), pltpu.VMEM((4, 1, 256), f32),
            regular, regular, regular, regular, regular, regular,
            dma, dma((4,)), dma, dma, dma((4,)), dma((4,)), dma, dma((2, 2)), dma, dma, dma((4,)), dma((3,)),
        ],
        compiler_params=pltpu.CompilerParams(
            collective_id=0, has_side_effects=True, vmem_limit_bytes=56 << 20
        ),
    )(slot_order.T, owner_of, gradients, moments, second_moments, factors.reshape(BLOCK, BLOCK))
    return direction, new_m, new_v, new_f[None, None]


def solution(mesh):
    split_blocks = P(None, "fsdp", "rep")
    return jax.shard_map(
        shards,
        mesh=mesh,
        in_specs=(split_blocks, split_blocks, split_blocks, P("fsdp", "rep", None, None), P(), P()),
        out_specs=(split_blocks, split_blocks, split_blocks, P("fsdp", "rep", None, None)),
        check_vma=False,
    )
```

time: 127 us -> 90.5 us (0.71)
  the two profiles are of different devices: /device:TPU:13 before, /device:TPU:3 now
where the time goes in v2:
time: 90.5 us; the launch traced here: 90.3 us
  Pallas kernels  84.2 us (93%)
  local copies, waits for them, and re-layouts  5.4 us (6%)
    pallas_call x1, Pallas kernels, shards(): pl.pallas_call(kernel, out_shape=(part, part, part, jax.ShapeDtypeStruct(...  84.2 us
    unnamed x8, local copies, waits for them, and re-layouts  5.4 us

profile of v2, /device:TPU:3, one launch (start us, length us, event | category | flops | bytes accessed | tf_op | source)
XLA Modules:
  0.0 90.3 jit_solution(7531678601333583273)
XLA Ops:
  0.6 84.2 %shard_map.93 = (f32[192,4,128]{2,1,0:T(4,128)}, f32[192,4,128]{2,1,0:T(4,128)}, f32[192,4,128]{2,1,0:T(4,128)}, f32[512,512]{1,0:T(8,128)}) custom-call(s32[2,128]{1,0:T(2,128)} %bitcast.5, s32[192]{0:T(256)} %owner_ref.1, f32[192,4,128]{2,1,0:T(4,128)} %g_ref.1, f32[192,4,128]{2,1,0:T(4,128)} %m_ref.1, f32[192,4,128]{2,1,0:T(4,128)} %v_ref.1, ...), custom_call_target="tpu_custom_call" | custom-call | tf_op jit(solution)/shard_map/pallas_call | solution.py:378
  84.9 0.0 copy-start
  84.9 1.9 %copy.14 = f32[192,4,128]{2,1,0:T(4,128)} copy(f32[192,4,128]{2,1,0:T(4,128)} %get-tuple-element.16) | data formatting | bytes 786432
  86.7 0.0 copy-start.1
  86.7 1.8 %copy.15 = f32[192,4,128]{2,1,0:T(4,128)} copy(f32[192,4,128]{2,1,0:T(4,128)} %get-tuple-element.17) | data formatting | bytes 786432
  88.5 0.0 copy-done.1
  88.6 0.7 copy.16
  89.3 0.0 copy-done
  89.3 1.0 %copy.17 = f32[1,1,512,512]{3,2,1,0:T(8,128)} copy(f32[1,1,512,512]{3,2,1,0:T(8,128)S(1)} %bitcast.4) | data formatting | bytes 2097152
Async XLA Ops:
  84.9 4.4 %copy-start = (f32[512,512]{1,0:T(8,128)S(1)}, f32[512,512]{1,0:T(8,128)}, u32[]{:S(2)}) copy-start(f32[512,512]{1,0:T(8,128)} %get-tuple-element.11) | copy-start | bytes 3145732
  86.7 1.8 %copy-start.1 = (f32[192,4,128]{2,1,0:T(4,128)S(1)}, f32[192,4,128]{2,1,0:T(4,128)}, u32[]{:S(2)}) copy-start(f32[192,4,128]{2,1,0:T(4,128)} %get-tuple-element.18) | copy-start | bytes 1179652

commit v3 on v2

--- a/solution.py
+++ b/solution.py
@@ -87,11 +87,12 @@
 
 
 def kernel(
-    slot_ref, owner_ref, g_ref, m_ref, v_ref, f_ref,
-    dir_ref, nm_ref, nv_ref, nf_ref,
+    slot_ref, owner_ref, g_hbm, m_hbm, v_hbm, f_hbm,
+    dir_hbm, nm_hbm, nv_hbm, nf_hbm,
+    g_ref, m_ref, v_ref, f_ref, dir_ref, nm_ref, nv_ref, nf_ref, where_ref,
     pay, gq, other, gram, xq, xs, ret, eye_ref, g_full, sums, part, ga, gz, gx,
     inside, stage2, stage3, stage4, go2, go3,
-    send1, recv1, fsend, frecv, usend, urecv, spsend, sprecv, send2, recv2, asend, arecv,
+    send1, recv1, fsend, frecv, usend, urecv, spsend, sprecv, send2, recv2, asend, arecv, loads, stores,
 ):
     me = lax.axis_index("fsdp")
     rep = lax.axis_index("rep")
@@ -116,11 +117,20 @@
             for s in range(1, 8):
                 signal(barrier, wrap(z + s, 8) * 16 + yc, wrap(rep + 2 * t, 4))
 
+    arrays = ((g_hbm, g_ref), (m_hbm, m_ref), (v_hbm, v_ref), (f_hbm, f_ref))
+    load = [pltpu.make_async_copy(a, b, loads.at[i]) for i, (a, b) in enumerate(arrays)]
+    arrays = ((dir_ref, dir_hbm), (nm_ref, nm_hbm), (nv_ref, nv_hbm), (nf_ref, nf_hbm))
+    store = [pltpu.make_async_copy(a, b, stores.at[i]) for i, (a, b) in enumerate(arrays)]
+    for copy in load:
+        copy.start()
+
     @pl.when(odd)
     def _():
         pl.semaphore_wait(barrier, 1)
-        remote(f_ref, other, fsend, frecv, (me, rep - 1)).start()
+        remote(f_hbm, other, fsend, frecv, (me, rep - 1)).start()
         signal(inside, me, rep - 1)
+
+    load[0].wait()
 
     def pick(o, carry):
         for k in range(2):
@@ -175,11 +185,15 @@
     def _():
         pl.semaphore_wait(go3, 1)
 
+    load[1].wait()
+    load[2].wait()
     grad = g_ref[...]
     new_m = MOMENT_DECAY * m_ref[...] + (1.0 - MOMENT_DECAY) * grad
     new_v = SECOND_DECAY * v_ref[...] + (1.0 - SECOND_DECAY) * grad * grad
     nm_ref[...] = new_m
     nv_ref[...] = new_v
+    store[1].start()
+    store[2].start()
     adam = new_m / (jnp.sqrt(new_v) + ADAM_EPSILON)
     rows = jnp.sum(adam * adam, axis=1)
     part[...] = jnp.zeros_like(part)
@@ -207,6 +221,14 @@
         return functools.reduce(lambda x, y: x + y, [buf[s] for s in range(n)])
 
     share(ga, 0, yc, 16, total, y_peer)
+    load[3].wait()
+
+    def locate(b, carry):
+        o = owner_ref[b]
+        where_ref[b] = o + OWNERS * jnp.where(slot_ref[0, o] == b, 0, 1)
+        return carry
+
+    lax.fori_loop(0, BLOCKS, locate, 0, unroll=8)
 
     def share_z():
         share(gz, 1, z, 8, shared(ga, 0, 16), z_peer)
@@ -268,11 +290,12 @@
         left_gram = mm(gs, gs, ((1,), (1,)))
         left = FACTOR_DECAY * f_ref[...] + (1.0 - FACTOR_DECAY) * left_gram
         nf_ref[...] = left
+        store[3].start()
         share_z()
         left_root = run(root_steps(left, eye_ref[...]))
         applied = split(mm(left_root, gs))
         share_x()
-        remote(f_ref, other, fsend, frecv, (me, rep + 1)).wait_recv()
+        remote(f_hbm, other, fsend, frecv, (me, rep + 1)).wait_recv()
         right = FACTOR_DECAY * other[...] + (1.0 - FACTOR_DECAY) * gram[...]
         right_root = run(root_steps(right, eye_ref[...]))
         shampoo = mm(applied, right_root)
@@ -296,19 +319,28 @@
         def own(d, same):
             chunk = xq.at[rep, d // 2, lax.rem(d, 2)]
             if same:
-                pltpu.make_async_copy(chunk, ret.at[slot, me], recv2).start()
+                pltpu.make_async_copy(chunk, ret.at[OWNERS * slot + me], recv2).start()
             else:
-                remote(chunk, ret.at[slot, me], send2, recv2, (d, rep)).start()
+                remote(chunk, ret.at[OWNERS * slot + me], send2, recv2, (d, rep)).start()
 
         def across(d, same):
-            remote(xq.at[twin, d // 2, lax.rem(d, 2)], ret.at[slot, me], send2, recv2, (d, twin)).start()
+            remote(xq.at[twin, d // 2, lax.rem(d, 2)], ret.at[OWNERS * slot + me], send2, recv2, (d, twin)).start()
 
         def aside(d, same):
             for c in (1, 3):
-                remote(xq.at[c, d // 2, lax.rem(d, 2)], ret.at[slot, me], send2, recv2, (d, c)).start()
-
-        each(range(8), own)
-        each(range(8), across)
+                remote(xq.at[c, d // 2, lax.rem(d, 2)], ret.at[OWNERS * slot + me], send2, recv2, (d, c)).start()
+
+        def everyone(act):
+            act(me, True)
+
+            def body(s, carry):
+                act(lax.rem(me + s * 37, OWNERS), False)
+                return carry
+
+            lax.fori_loop(1, OWNERS, body, 0, unroll=4)
+
+        everyone(own)
+        everyone(across)
         each(DIRECT, aside)
         units(RELAYED, spsend)
         units(127 + 16 * len(DIRECT), send2)
@@ -325,13 +357,11 @@
                 a, b = slice(128 * i, 128 * i + 128), slice(128 * j, 128 * j + 128)
                 square = other[a, b] if i <= j else other[b, a].T
                 nf_ref[a, b] = FACTOR_DECAY * f_ref[a, b] + (1.0 - FACTOR_DECAY) * square
+        store[3].start()
 
         def give(d, same):
-            chunk = xs.at[:, d // 2, lax.rem(d, 2)]
-            if same:
-                pltpu.make_async_copy(chunk, ret.at[:, me], recv2).start()
-            else:
-                remote(chunk, ret.at[:, me], send2, recv2, (d, rep)).start()
+            for k in range(2):
+                remote(xs.at[k, d // 2, lax.rem(d, 2)], ret.at[OWNERS * k + me], send2, recv2, (d, rep)).start()
 
         for phase, dzs in enumerate(PHASES):
             some = xs.at[0, pl.ds(0, 8 * len(dzs))]
@@ -341,7 +371,7 @@
         units(RELAYED, send2)
         pair = gx.at[pl.ds(0, 2)]
         pltpu.make_async_copy(pair, pair, asend.at[2]).wait()
-        remote(f_ref, other, fsend, frecv, (me, rep - 1)).wait_send()
+        remote(f_hbm, other, fsend, frecv, (me, rep - 1)).wait_send()
 
     pltpu.make_async_copy(pay.at[:, pl.ds(0, 127)], pay.at[:, pl.ds(0, 127)], send1).wait()
     for k in range(2):
@@ -352,12 +382,11 @@
     pltpu.make_async_copy(ret, ret, recv2).wait()
 
     def place(b, carry):
-        o = owner_ref[b]
-        k = jnp.where(slot_ref[0, o] == b, 0, 1)
-        dir_ref[b] = ret[k, o]
+        dir_ref[b] = ret[where_ref[b]]
         return carry
 
     lax.fori_loop(0, BLOCKS, place, 0, unroll=8)
+    store[0].start()
 
     @pl.when(site)
     def _():
@@ -365,9 +394,32 @@
             panel = gram.at[pl.ds(128 * i, 128), pl.ds(128 * i, BLOCK - 128 * i)]
             remote(panel, panel, usend.at[i], urecv.at[i], (me, rep + 1)).wait_send()
 
+    for copy in store:
+        copy.wait()
+
+
+def pass_on(*refs):
+    sources, results, held, sems = refs[:4], refs[4:8], refs[8:12], refs[12]
+    arriving, leaving = [], []
+    for i in range(4):
+        half = sources[i].shape[0] // 2
+        for h in range(2):
+            rows = pl.ds(h * half, half)
+            arriving.append(pltpu.make_async_copy(sources[i].at[rows], held[i].at[rows], sems.at[2 * i + h, 0]))
+            leaving.append(pltpu.make_async_copy(held[i].at[rows], results[i].at[rows], sems.at[2 * i + h, 1]))
+    for copy in arriving:
+        copy.start()
+    for come, go in zip(arriving, leaving):
+        come.wait()
+        go.start()
+    for copy in leaving:
+        copy.wait()
+
 
 def shards(gradients, moments, second_moments, factors, owner_of, slot_order):
-    vmem = pl.BlockSpec(memory_space=pltpu.VMEM)
+    anywhere = pl.BlockSpec(memory_space=pl.ANY)
+    blocks = pltpu.VMEM((BLOCKS, 4, 128), f32)
+    chunks2 = pltpu.VMEM((2 * OWNERS, 4, 128), f32)
     smem = pl.BlockSpec(memory_space=pltpu.SMEM)
     part = jax.ShapeDtypeStruct(gradients.shape, f32)
     chunks = lambda n: pltpu.VMEM((n, OWNERS, 4, 128), f32)
@@ -375,22 +427,32 @@
     square = pltpu.VMEM((BLOCK, BLOCK), f32)
     dma = pltpu.SemaphoreType.DMA
     regular = pltpu.SemaphoreType.REGULAR
-    direction, new_m, new_v, new_f = pl.pallas_call(
+    out_shape = (part, part, part, jax.ShapeDtypeStruct((BLOCK, BLOCK), f32))
+    results = pl.pallas_call(
         kernel,
-        out_shape=(part, part, part, jax.ShapeDtypeStruct((BLOCK, BLOCK), f32)),
-        in_specs=[smem, smem, vmem, vmem, vmem, vmem],
-        out_specs=(vmem, vmem, vmem, vmem),
+        out_shape=out_shape,
+        in_specs=[smem, smem] + [anywhere] * 4,
+        out_specs=(anywhere,) * 4,
         scratch_shapes=[
-            chunks(2), halves(4), square, square, halves(4), halves(2), chunks(2), square, square,
+            blocks, blocks, blocks, square, blocks, blocks, blocks, square, pltpu.SMEM((BLOCKS,), jnp.int32),
+            chunks(2), halves(4), square, square, halves(4), halves(2), chunks2, square, square,
             pltpu.VMEM((1, 256), f32), pltpu.VMEM((256, 128), f32),
             pltpu.VMEM((16, 1, 256), f32), pltpu.VMEM((8, 1, 256), f32), pltpu.VMEM((4, 1, 256), f32),
             regular, regular, regular, regular, regular, regular,
             dma, dma((4,)), dma, dma, dma((4,)), dma((4,)), dma, dma((2, 2)), dma, dma, dma((4,)), dma((3,)),
+            dma((4,)), dma((4,)),
         ],
         compiler_params=pltpu.CompilerParams(
             collective_id=0, has_side_effects=True, vmem_limit_bytes=56 << 20
         ),
     )(slot_order.T, owner_of, gradients, moments, second_moments, factors.reshape(BLOCK, BLOCK))
+    direction, new_m, new_v, new_f = pl.pallas_call(
+        pass_on,
+        out_shape=out_shape,
+        in_specs=[anywhere] * 4,
+        out_specs=(anywhere,) * 4,
+        scratch_shapes=[blocks, blocks, blocks, square, dma((8, 2))],
+    )(*results)
     return direction, new_m, new_v, new_f[None, None]
 
 

time: 90.5 us -> 86.1 us (0.951)
  local copies, waits for them, and re-layouts: 5.4 us -> 0 us
  Pallas kernels: 84.2 us -> 85.3 us
    unnamed x8 -> x0, local copies, waits for them, and re-layouts: 5.4 us -> none
    pallas_call x1 -> x2, Pallas kernels: 84.2 us -> 85.3 us  [the longest x1 82.7 us: shards(): pl.pallas_call(kernel, out_shape=out_shape, in_specs=[smem, smem] + [anyw...]
where the time goes in v3:
time: 86.1 us; the launch traced here: 85.9 us
  Pallas kernels  85.3 us (99%)
    pallas_call x1, Pallas kernels, shards(): pl.pallas_call(kernel, out_shape=out_shape, in_specs=[smem, smem] + [anyw...  82.7 us
    pallas_call x1, Pallas kernels, shards(): pl.pallas_call(pass_on, out_shape=out_shape, in_specs=[anywhere] * 4, out...  2.62 us

profile of v3, /device:TPU:3, one launch (start us, length us, event | category | flops | bytes accessed | tf_op | source)
XLA Modules:
  0.0 85.9 jit_solution(6447522032991722483)
XLA Ops:
  0.6 82.7 %shard_map.93 = (f32[192,4,128]{2,1,0:T(4,128)}, f32[192,4,128]{2,1,0:T(4,128)}, f32[192,4,128]{2,1,0:T(4,128)}, f32[512,512]{1,0:T(8,128)}) custom-call(s32[2,128]{1,0:T(2,128)} %bitcast.4, s32[192]{0:T(256)} %owner_ref.1, f32[192,4,128]{2,1,0:T(4,128)} %g_hbm.1, f32[192,4,128]{2,1,0:T(4,128)} %m_hbm.1, f32[192,4,128]{2,1,0:T(4,128)} %v_hbm.1, ...), custom_call_target="tpu_custom_call" | custom-call | tf_op jit(solution)/shard_map/pallas_call | solution.py:431
  83.3 2.6 %shard_map.94 = (f32[192,4,128]{2,1,0:T(4,128)}, f32[192,4,128]{2,1,0:T(4,128)}, f32[192,4,128]{2,1,0:T(4,128)}, f32[512,512]{1,0:T(8,128)}) custom-call(f32[192,4,128]{2,1,0:T(4,128)} %get-tuple-element.12.refs_0_, f32[192,4,128]{2,1,0:T(4,128)} %get-tuple-element.13.refs_1_, f32[192,4,128]{2,1,0:T(4,128)} %get-tuple-element.14.refs_2_, ...), custom_call_target="tpu_custom_call" | custom-call | tf_op jit(solution)/shard_map/pallas_call | solution.py:449

commit v4 on v3

--- a/solution.py
+++ b/solution.py
@@ -19,6 +19,7 @@
 BLOCKS = 192
 MESH = pl.DeviceIdType.MESH
 DIRECT = (0, 4)
+EARLY = 320
 PHASES = ((1, 2, 3), (5, 6, 7))
 RELAYED = 16 * sum(len(p) for p in PHASES)
 f32 = jnp.float32
@@ -91,13 +92,16 @@
     dir_hbm, nm_hbm, nv_hbm, nf_hbm,
     g_ref, m_ref, v_ref, f_ref, dir_ref, nm_ref, nv_ref, nf_ref, where_ref,
     pay, gq, other, gram, xq, xs, ret, eye_ref, g_full, sums, part, ga, gz, gx,
-    inside, stage2, stage3, stage4, go2, go3,
+    inside, more, stage2, stage3, stage4, go2, go3,
     send1, recv1, fsend, frecv, usend, urecv, spsend, sprecv, send2, recv2, asend, arecv, loads, stores,
 ):
     me = lax.axis_index("fsdp")
     rep = lax.axis_index("rep")
     z = me // 16
     yc = me - z * 16
+    chip = me // 2
+    core = me - 2 * chip
+    y = chip - 8 * z
     site = lax.rem(rep, 2) == 0
     odd = jnp.logical_not(site)
     slot = rep // 2
@@ -124,10 +128,14 @@
     for copy in load:
         copy.start()
 
+    def factor(part, there):
+        rows = pl.ds(0, EARLY) if part == 0 else pl.ds(EARLY, BLOCK - EARLY)
+        return remote(f_hbm.at[rows], other.at[rows], fsend.at[part], frecv.at[part], (me, there))
+
     @pl.when(odd)
     def _():
         pl.semaphore_wait(barrier, 1)
-        remote(f_hbm, other, fsend, frecv, (me, rep - 1)).start()
+        factor(0, rep - 1).start()
         signal(inside, me, rep - 1)
 
     load[0].wait()
@@ -154,15 +162,16 @@
     def _():
         pl.semaphore_wait(go2, 1)
 
-    def send(s, carry):
-        d = lax.rem(me + s * 37, OWNERS)
+    own_chunk = gq.at[rep, chip, core]
+
+    def send(s, d):
+        d = wrap(d + 37, OWNERS)
         for k in range(2):
-            remote(pay.at[k, d], gq.at[rep, me // 2, lax.rem(me, 2)], send1, recv1.at[rep], (d, 2 * k)).start()
-        return carry
-
-    lax.fori_loop(1, OWNERS, send, 0, unroll=4)
+            remote(pay.at[k, d], own_chunk, send1, recv1.at[rep], (d, 2 * k)).start()
+        return d
+
+    lax.fori_loop(1, OWNERS, send, me, unroll=4)
     for k in range(2):
-        own_chunk = gq.at[rep, me // 2, lax.rem(me, 2)]
 
         @pl.when(rep != 2 * k)
         def _():
@@ -261,15 +270,29 @@
 
     def each(dzs, act):
         for dz in dzs:
-            base = wrap(z + dz, 8) * 16
+            base = wrap(z + dz, 8) * 8
             if dz == 0:
-                act(me, True)
+                act(chip, core, True)
+                act(chip, 1 - core, False)
 
             def body(j, carry):
-                act(base + wrap(yc + j, 16), False)
+                for c in range(2):
+                    act(base + wrap(y + j, 8), c, False)
                 return carry
 
-            lax.fori_loop(1 if dz == 0 else 0, 16, body, 0, unroll=4 if dz else 3)
+            lax.fori_loop(0 if dz else 1, 8, body, 0, unroll=4 if dz else 7)
+
+    def everyone(act):
+        act(chip, core, True)
+        act(chip, 1 - core, False)
+
+        def body(s, e):
+            e = wrap(e + 37, 64)
+            for c in range(2):
+                act(e, c, False)
+            return e
+
+        lax.fori_loop(1, 64, body, chip, unroll=3)
 
     @pl.when(site)
     def _():
@@ -278,6 +301,7 @@
         eye_ref[...] = jnp.where(row == col, 1.0, 0.0)
         for q in range(4):
             pltpu.make_async_copy(gq.at[q], gq.at[q], recv1.at[q]).wait()
+        signal(more, me, rep + 1)
         for q in range(4):
             both = jnp.concatenate([gq[q, :, 0], gq[q, :, 1]], axis=1)
             g_full[:, q * 128 : (q + 1) * 128] = both.reshape(BLOCK, 128)
@@ -295,7 +319,8 @@
         left_root = run(root_steps(left, eye_ref[...]))
         applied = split(mm(left_root, gs))
         share_x()
-        remote(f_hbm, other, fsend, frecv, (me, rep + 1)).wait_recv()
+        factor(0, rep + 1).wait_recv()
+        factor(1, rep + 1).wait_recv()
         right = FACTOR_DECAY * other[...] + (1.0 - FACTOR_DECAY) * gram[...]
         right_root = run(root_steps(right, eye_ref[...]))
         shampoo = mm(applied, right_root)
@@ -316,28 +341,20 @@
                 for c in (1, 3):
                     remote(xq.at[c, group(dz)], xs.at[slot, group(dz)], spsend, sprecv.at[slot, phase], (me, c)).start()
 
-        def own(d, same):
-            chunk = xq.at[rep, d // 2, lax.rem(d, 2)]
+        place_there = ret.at[OWNERS * slot + me]
+
+        def own(e, c, same):
             if same:
-                pltpu.make_async_copy(chunk, ret.at[OWNERS * slot + me], recv2).start()
+                pltpu.make_async_copy(xq.at[rep, e, c], place_there, recv2).start()
             else:
-                remote(chunk, ret.at[OWNERS * slot + me], send2, recv2, (d, rep)).start()
-
-        def across(d, same):
-            remote(xq.at[twin, d // 2, lax.rem(d, 2)], ret.at[OWNERS * slot + me], send2, recv2, (d, twin)).start()
-
-        def aside(d, same):
-            for c in (1, 3):
-                remote(xq.at[c, d // 2, lax.rem(d, 2)], ret.at[OWNERS * slot + me], send2, recv2, (d, c)).start()
-
-        def everyone(act):
-            act(me, True)
-
-            def body(s, carry):
-                act(lax.rem(me + s * 37, OWNERS), False)
-                return carry
-
-            lax.fori_loop(1, OWNERS, body, 0, unroll=4)
+                remote(xq.at[rep, e, c], place_there, send2, recv2, (2 * e + c, rep)).start()
+
+        def across(e, c, same):
+            remote(xq.at[twin, e, c], place_there, send2, recv2, (2 * e + c, twin)).start()
+
+        def aside(e, c, same):
+            for q in (1, 3):
+                remote(xq.at[q, e, c], place_there, send2, recv2, (2 * e + c, q)).start()
 
         everyone(own)
         everyone(across)
@@ -349,6 +366,8 @@
 
     @pl.when(odd)
     def _():
+        pl.semaphore_wait(more, 1)
+        factor(1, rep - 1).start()
         for i in range(4):
             there = other.at[pl.ds(128 * i, 128), pl.ds(128 * i, BLOCK - 128 * i)]
             remote(there, there, usend.at[i], urecv.at[i], (me, rep - 1)).wait_recv()
@@ -359,9 +378,9 @@
                 nf_ref[a, b] = FACTOR_DECAY * f_ref[a, b] + (1.0 - FACTOR_DECAY) * square
         store[3].start()
 
-        def give(d, same):
+        def give(e, c, same):
             for k in range(2):
-                remote(xs.at[k, d // 2, lax.rem(d, 2)], ret.at[OWNERS * k + me], send2, recv2, (d, rep)).start()
+                remote(xs.at[k, e, c], ret.at[OWNERS * k + me], send2, recv2, (2 * e + c, rep)).start()
 
         for phase, dzs in enumerate(PHASES):
             some = xs.at[0, pl.ds(0, 8 * len(dzs))]
@@ -371,7 +390,8 @@
         units(RELAYED, send2)
         pair = gx.at[pl.ds(0, 2)]
         pltpu.make_async_copy(pair, pair, asend.at[2]).wait()
-        remote(f_hbm, other, fsend, frecv, (me, rep - 1)).wait_send()
+        factor(0, rep - 1).wait_send()
+        factor(1, rep - 1).wait_send()
 
     pltpu.make_async_copy(pay.at[:, pl.ds(0, 127)], pay.at[:, pl.ds(0, 127)], send1).wait()
     for k in range(2):
@@ -438,8 +458,8 @@
             chunks(2), halves(4), square, square, halves(4), halves(2), chunks2, square, square,
             pltpu.VMEM((1, 256), f32), pltpu.VMEM((256, 128), f32),
             pltpu.VMEM((16, 1, 256), f32), pltpu.VMEM((8, 1, 256), f32), pltpu.VMEM((4, 1, 256), f32),
-            regular, regular, regular, regular, regular, regular,
-            dma, dma((4,)), dma, dma, dma((4,)), dma((4,)), dma, dma((2, 2)), dma, dma, dma((4,)), dma((3,)),
+            regular, regular, regular, regular, regular, regular, regular,
+            dma, dma((4,)), dma((2,)), dma((2,)), dma((4,)), dma((4,)), dma, dma((2, 2)), dma, dma, dma((4,)), dma((3,)),
             dma((4,)), dma((4,)),
         ],
         compiler_params=pltpu.CompilerParams(

time: 86.1 us -> 82.3 us (0.956)
  Pallas kernels: 85.3 us -> 81.5 us
    pallas_call x1, Pallas kernels: 82.7 us -> 78.9 us  [shards(): pl.pallas_call(kernel, out_shape=out_shape, in_specs=[smem, smem] + [anyw...]
where the time goes in v4:
time: 82.3 us; the launch traced here: 82.1 us
  Pallas kernels  81.5 us (99%)
    pallas_call x1, Pallas kernels, shards(): pl.pallas_call(kernel, out_shape=out_shape, in_specs=[smem, smem] + [anyw...  78.9 us
    pallas_call x1, Pallas kernels, shards(): pl.pallas_call(pass_on, out_shape=out_shape, in_specs=[anywhere] * 4, out...  2.62 us

profile of v4, /device:TPU:3, one launch (start us, length us, event | category | flops | bytes accessed | tf_op | source)
XLA Modules:
  0.0 82.1 jit_solution(14309062148505032638)
XLA Ops:
  0.6 78.9 %shard_map.93 = (f32[192,4,128]{2,1,0:T(4,128)}, f32[192,4,128]{2,1,0:T(4,128)}, f32[192,4,128]{2,1,0:T(4,128)}, f32[512,512]{1,0:T(8,128)}) custom-call(s32[2,128]{1,0:T(2,128)} %bitcast.4, s32[192]{0:T(256)} %owner_ref.1, f32[192,4,128]{2,1,0:T(4,128)} %g_hbm.1, f32[192,4,128]{2,1,0:T(4,128)} %m_hbm.1, f32[192,4,128]{2,1,0:T(4,128)} %v_hbm.1, ...), custom_call_target="tpu_custom_call" | custom-call | tf_op jit(solution)/shard_map/pallas_call | solution.py:451
  79.5 2.6 %shard_map.94 = (f32[192,4,128]{2,1,0:T(4,128)}, f32[192,4,128]{2,1,0:T(4,128)}, f32[192,4,128]{2,1,0:T(4,128)}, f32[512,512]{1,0:T(8,128)}) custom-call(f32[192,4,128]{2,1,0:T(4,128)} %get-tuple-element.12.refs_0_, f32[192,4,128]{2,1,0:T(4,128)} %get-tuple-element.13.refs_1_, f32[192,4,128]{2,1,0:T(4,128)} %get-tuple-element.14.refs_2_, ...), custom_call_target="tpu_custom_call" | custom-call | tf_op jit(solution)/shard_map/pallas_call | solution.py:469

commit v5 on v4

--- a/solution.py
+++ b/solution.py
@@ -19,7 +19,7 @@
 BLOCKS = 192
 MESH = pl.DeviceIdType.MESH
 DIRECT = (0, 4)
-EARLY = 320
+EARLY = 256
 PHASES = ((1, 2, 3), (5, 6, 7))
 RELAYED = 16 * sum(len(p) for p in PHASES)
 f32 = jnp.float32

time: 82.3 us -> 85.1 us (1.034)
  Pallas kernels: 81.5 us -> 84.3 us
    pallas_call x1, Pallas kernels: 78.9 us -> 81.7 us  [shards(): pl.pallas_call(kernel, out_shape=out_shape, in_specs=[smem, smem] + [anyw...]
where the time goes in v5:
time: 85.1 us; the launch traced here: 85 us
  Pallas kernels  84.3 us (99%)
    pallas_call x1, Pallas kernels, shards(): pl.pallas_call(kernel, out_shape=out_shape, in_specs=[smem, smem] + [anyw...  81.7 us
    pallas_call x1, Pallas kernels, shards(): pl.pallas_call(pass_on, out_shape=out_shape, in_specs=[anywhere] * 4, out...  2.62 us

profile of v5, /device:TPU:3, one launch (start us, length us, event | category | flops | bytes accessed | tf_op | source)
XLA Modules:
  0.0 85.0 jit_solution(5694991721483312498)
XLA Ops:
  0.6 81.7 %shard_map.93 = (f32[192,4,128]{2,1,0:T(4,128)}, f32[192,4,128]{2,1,0:T(4,128)}, f32[192,4,128]{2,1,0:T(4,128)}, f32[512,512]{1,0:T(8,128)}) custom-call(s32[2,128]{1,0:T(2,128)} %bitcast.4, s32[192]{0:T(256)} %owner_ref.1, f32[192,4,128]{2,1,0:T(4,128)} %g_hbm.1, f32[192,4,128]{2,1,0:T(4,128)} %m_hbm.1, f32[192,4,128]{2,1,0:T(4,128)} %v_hbm.1, ...), custom_call_target="tpu_custom_call" | custom-call | tf_op jit(solution)/shard_map/pallas_call | solution.py:451
  82.3 2.6 %shard_map.94 = (f32[192,4,128]{2,1,0:T(4,128)}, f32[192,4,128]{2,1,0:T(4,128)}, f32[192,4,128]{2,1,0:T(4,128)}, f32[512,512]{1,0:T(8,128)}) custom-call(f32[192,4,128]{2,1,0:T(4,128)} %get-tuple-element.12.refs_0_, f32[192,4,128]{2,1,0:T(4,128)} %get-tuple-element.13.refs_1_, f32[192,4,128]{2,1,0:T(4,128)} %get-tuple-element.14.refs_2_, ...), custom_call_target="tpu_custom_call" | custom-call | tf_op jit(solution)/shard_map/pallas_call | solution.py:469
